TPU v7x, 256 devices: a whole 4x4x8 slice. The times are simulated.
256 devices in a mesh: blk: 64 (over z, y, core), rep: 4 (over x).
Axes of the slice: x: 4, y: 4, z: 8, core: 2. Of those that a mesh axis runs over, the one named last changes fastest.
Arguments:
- embeddings: bfloat16 [524288, 1024], P(('blk', 'rep'))
- destination: int32 [524288], P(('blk', 'rep')), may hold values from 0 to 524287, as said below
- arrival: int32 [524288], P(('blk', 'rep')), may hold values from 0 to 3071, as said below
- dataset_index: int32 [524288], replicated, may hold values from 0 to 524287, each once
Outputs:
- best_similarity: float32 [524288], P(('blk', 'rep'))
Inputs may be any that keep to these rules, and one draw needn't show every extreme that they name: A permutation. The rows of one source block of 2048 rows go to 256 target blocks destination // 2048 (all blocks when 2 * 128 equals their number), with any index along rep; no source block sends more than 12 rows to one target block, and every source block sends exactly 12 to some. Consistent with destination: the row named by arrival[p] is the stored row whose destination is p.
All inputs are finite; a program needn't handle non-finite values.
Results may differ from a plain program's by a relative error of at most 0.00043.
Values may be sent and summed in bfloat16 or wider, within the bound.
A program may use at most 64 MiB of HBM per device.

v0:
```python
import math

import jax
import jax.numpy as jnp
from jax import lax
from jax.sharding import PartitionSpec as P


def swapped(x, axis, apart):
    return lax.ppermute(x, axis, [(i, i ^ 1 << apart) for i in range(lax.axis_size(axis))])


def normalize(raw_rows):
    widened = raw_rows.astype(jnp.float32)
    row_scale = lax.rsqrt(jnp.mean(widened * widened, axis=1, keepdims=True) + 1e-06) / math.sqrt(
        widened.shape[1]
    )
    return (widened * row_scale).astype(jnp.bfloat16)


def masked_tile(left_rows, left_rank, right_rows, right_rank):
    scores = lax.dot_general(
        left_rows, right_rows, (((1,), (1,)), ((), ())), preferred_element_type=jnp.float32
    )
    earlier = right_rank[None, :] < left_rank[:, None]
    row_best = jnp.max(jnp.where(earlier, scores, jnp.float32(-1.0)), axis=1)
    col_best = jnp.max(jnp.where(earlier, jnp.float32(-1.0), scores), axis=0)
    return (row_best, col_best)


def on_device(embeddings, destination, arrival, dataset_index):
    rows_dev = embeddings.shape[0]
    features = embeddings.shape[1]
    blk_count = lax.axis_size("blk")
    rep_count = lax.axis_size("rep")
    devices = blk_count * rep_count
    spread = min(devices // 2, rows_dev // 4)
    capacity = 3 * rows_dev // (4 * spread)
    normal_rows = normalize(embeddings)
    target = destination // rows_dev
    onehot = (target[:, None] == jnp.arange(devices, dtype=jnp.int32)[None, :]).astype(jnp.int32)
    within = jnp.sum((jnp.cumsum(onehot, axis=0) - 1) * onehot, axis=1)
    slot_index = target * capacity + within
    source_of = (
        jnp.zeros((devices * capacity,), jnp.int32)
        .at[slot_index]
        .set(jnp.arange(rows_dev, dtype=jnp.int32))
    )
    filled = jnp.zeros((devices * capacity,), jnp.int32).at[slot_index].set(1)
    outbound_rows = jnp.where(
        filled[:, None] == 1, normal_rows[source_of], jnp.zeros((), jnp.bfloat16)
    )
    outbound_rows = outbound_rows.reshape(blk_count, rep_count, capacity, features)
    received = lax.all_to_all(
        lax.all_to_all(outbound_rows, "blk", split_axis=0, concat_axis=0, tiled=True),
        "rep",
        split_axis=1,
        concat_axis=1,
        tiled=True,
    )
    cluster_block = received.reshape(devices * capacity, features)[arrival]
    blk_index = lax.axis_index("blk")
    rep_index = lax.axis_index("rep")
    parity = blk_index % 2
    own_block_id = blk_index * rep_count + rep_index
    partner_id = own_block_id + rep_count * (1 - 2 * parity)
    own_rank = lax.dynamic_slice_in_dim(dataset_index, own_block_id * rows_dev, rows_dev)
    partner_rank = lax.dynamic_slice_in_dim(dataset_index, partner_id * rows_dev, rows_dev)
    partner = swapped(cluster_block, "blk", 0)
    diagonal = masked_tile(cluster_block, own_rank, cluster_block, own_rank)[0]
    cross_best = masked_tile(cluster_block, own_rank, partner, partner_rank)[0]
    return jnp.maximum(diagonal, cross_best)


def solution(mesh):
    placed = (P(("blk", "rep"), None), P(("blk", "rep")), P(("blk", "rep")), P())
    return jax.shard_map(
        on_device, mesh=mesh, in_specs=placed, out_specs=P(("blk", "rep")), check_vma=False
    )
```

profile of v0, /device:TPU:1, one launch (start us, length us, event | category | flops | bytes accessed | tf_op | source)
XLA Modules:
  0.0 378.6 jit_solution(14712078338764350947)
XLA Ops:
  0.0 0.7 add_select_fusion
  0.7 0.1 copy.7
  0.8 0.3 fusion.3
  1.2 0.3 add_add_fusion
  1.5 0.0 copy-start.2
  1.5 1.2 copy.8
  2.7 0.9 fusion.2
  3.7 8.1 %scatter_custom_fusion.1 = s32[3072]{0:T(1024)S(1)} fusion(s32[2048]{0:T(1024)S(1)} %compare_select_fusion.2, s32[2048]{0:T(1024)S(1)} %iota.11, s32[]{:T(128)} %constant.58.clone.1), kind=kCustom, calls=%fused_computation.34 | custom fusion | bytes 12292 | tf_op jit(solution)/shard_map/scatter | solution.py:47
  11.7 0.0 copy-start
  11.7 3.2 fusion
  15.0 0.2 copy-done
  15.2 2.7 fusion.1
  17.8 18.7 %gather_fusion = bf16[3072,1024]{1,0:T(8,128)(2,1)} fusion(bf16[2048,1024]{1,0:T(8,128)(2,1)} %fusion.1, s32[3072]{0:T(1024)S(1)} %fusion.6), kind=kCustom, calls=%fused_computation | custom fusion | bytes 12595200 | tf_op jit(solution)/shard_map/gather | solution.py:51
  36.5 10.6 %gather.9 = bf16[64,4,12,1024]{3,2,1,0:T(8,128)(2,1)} reshape(bf16[3072,1024]{1,0:T(8,128)(2,1)} %gather_fusion) | data formatting | bytes 12582912 | tf_op jit(solution)/shard_map/gather | solution.py:51
  47.1 8.1 %scatter_custom_fusion = s32[3072]{0:T(1024)S(1)} fusion(s32[2048]{0:T(1024)S(1)} %compare_select_fusion.2, s32[2048]{0:T(1024)S(1)} %ne.20, s32[]{:T(128)} %constant.58.clone.1), kind=kCustom, calls=%fused_computation.36 | custom fusion | bytes 12292 | tf_op jit(solution)/shard_map/scatter | solution.py:49
  55.2 0.2 broadcast_in_dim.39
  55.3 7.7 %broadcast_select_fusion = bf16[64,4,12,1024]{3,2,1,0:T(8,128)(2,1)} fusion(bf16[64,4,12,1024]{3,2,1,0:T(8,128)(2,1)} %gather.9, pred[64,4,12]{2,1,0:T(4,128)(4,1)S(1)} %broadcast_in_dim.39), kind=kLoop, calls=%fused_computation.10 | loop fusion | flops 3145728 | bytes 12585984 | tf_op jit(solution)/shard_map/jit(_where)/select_n | solution.py:50
  63.0 18.8 %copy.9 = bf16[64,4,12,1024]{3,1,2,0:T(4,128)(2,1)} copy(bf16[64,4,12,1024]{3,2,1,0:T(8,128)(2,1)} %broadcast_select_fusion) | data formatting | bytes 12582912 | tf_op jit(solution)/shard_map/jit(_where)/select_n | solution.py:50
  81.8 152.7 %all_to_all.10 = bf16[64,4,12,1024]{3,1,2,0:T(4,128)(2,1)S(1)} all-to-all(bf16[64,4,12,1024]{3,1,2,0:T(4,128)(2,1)} %copy.9), channel_id=1, replica_groups=mesh['blk'=64,'rep'=4] {'blk'}, dimensions={0} | all-to-all | bytes 12582912 | tf_op jit(solution)/shard_map/all_to_all | solution.py:55
  234.5 6.2 %copy.10 = bf16[64,4,12,1024]{3,0,2,1:T(8,128)(2,1)} copy(bf16[64,4,12,1024]{3,1,2,0:T(4,128)(2,1)S(1)} %all_to_all.10) | data formatting | bytes 12582912 | tf_op jit(solution)/shard_map/all_to_all | solution.py:55
  240.8 5.4 %all-to-all-start.1 = ((bf16[64,4,12,1024]{3,0,2,1:T(8,128)(2,1)}), bf16[64,4,12,1024]{3,0,2,1:T(8,128)(2,1)}, u32[]{:S(2)}, u32[]{:S(2)}) async-start(bf16[64,4,12,1024]{3,0,2,1:T(8,128)(2,1)} %copy.10), calls=%async_computation.1 | async-start | bytes 12582912 | tf_op jit(solution)/shard_map/all_to_all | solution.py:54
  246.2 69.2 %all-to-all-done.1 = bf16[64,4,12,1024]{3,0,2,1:T(8,128)(2,1)} async-done(((bf16[64,4,12,1024]{3,0,2,1:T(8,128)(2,1)}), bf16[64,4,12,1024]{3,0,2,1:T(8,128)(2,1)}, u32[]{:S(2)}, u32[]{:S(2)}) %all-to-all-start.1) | async-done | bytes 6291488 | tf_op jit(solution)/shard_map/all_to_all | solution.py:54
  315.4 9.8 %copy.11 = bf16[64,4,12,1024]{3,2,1,0:T(8,128)(2,1)} copy(bf16[64,4,12,1024]{3,0,2,1:T(8,128)(2,1)} %all-to-all-done.1) | data formatting | bytes 12582912 | tf_op jit(solution)/shard_map/all_to_all | solution.py:54
  325.2 10.7 %reshape.44 = bf16[3072,1024]{1,0:T(8,128)(2,1)} reshape(bf16[64,4,12,1024]{3,2,1,0:T(8,128)(2,1)} %copy.11) | data formatting | bytes 12582912 | tf_op jit(solution)/shard_map/reshape | solution.py:61
  335.9 14.6 %gather_fusion.1 = bf16[2048,1024]{1,0:T(8,128)(2,1)} fusion(bf16[3072,1024]{1,0:T(8,128)(2,1)} %reshape.44, s32[2048]{0:T(1024)S(1)} %fusion.8), kind=kCustom, calls=%fused_computation.1 | custom fusion | bytes 8396800 | tf_op jit(solution)/shard_map/gather | solution.py:61
  350.5 3.3 collective-permute-start
  353.7 0.7 fusion.15
  354.5 12.4 %select_reduce_fusion.1 = f32[2048]{0:T(1024)S(1)} fusion(s32[2048]{0:T(1024)S(1)} %get-tuple-element.6, bf16[2048,1024]{1,0:T(8,128)(2,1)} %gather_fusion.1), kind=kOutput, calls=%fused_computation.5 | convolution fusion | flops 8602515456 | bytes 4210688 | tf_op jit(solution)/shard_map/dot_general | solution.py:22
  366.9 0.0 collective-permute-done
  366.9 0.0 copy-done.1
  366.9 10.8 %select_reduce_fusion = f32[2048]{0:T(1024)S(1)} fusion(s32[2048]{0:T(1024)S(1)} %get-tuple-element.6, s32[2048]{0:T(1024)S(1)} %get-tuple-element.5, bf16[2048,1024]{1,0:T(8,128)(2,1)S(1)} %copy-done.1, bf16[2048,1024]{1,0:T(8,128)(2,1)} %collective-permute-done), kind=kOutput, calls=%fused_computation.4 | convolution fusion | flops 8602515456 | bytes 8413184 | tf_op jit(solution)/shard_map/dot_general | solution.py:22
  377.7 0.6 max.3
  (14 shorter events, 0.1 us)
Async XLA Ops:
  1.5 2.1 copy-start.2
  11.7 3.5 copy-start
  240.8 5.5 %copy-start.3 = (s32[2048]{0:T(1024)S(1)}, s32[2048]{0:T(1024)}, u32[]{:S(2)}) copy-start(s32[2048]{0:T(1024)} %param.6) | copy-start | bytes 24580
  240.8 74.7 %all-to-all-start.1 = ((bf16[64,4,12,1024]{3,0,2,1:T(8,128)(2,1)}), bf16[64,4,12,1024]{3,0,2,1:T(8,128)(2,1)}, u32[]{:S(2)}, u32[]{:S(2)}) async-start(bf16[64,4,12,1024]{3,0,2,1:T(8,128)(2,1)} %copy.10), calls=%async_computation.1 | async-start | bytes 12582912 | tf_op jit(solution)/shard_map/all_to_all | solution.py:54
  350.5 16.4 %collective-permute-start = (bf16[2048,1024]{1,0:T(8,128)(2,1)}, bf16[2048,1024]{1,0:T(8,128)(2,1)}, u32[]{:S(2)}, u32[]{:S(2)}) collective-permute-start(bf16[2048,1024]{1,0:T(8,128)(2,1)} %gather_fusion.1), channel_id=1, source_target_pairs={{0,4},{4,0},{8,12},{12,8},{16,20},{20,16},{24,28},{28,24},{32,36},... | collective-permute-start | bytes 12582920 | tf_op jit(solution)/shard_map/ppermute | solution.py:10
  354.5 12.4 %copy-start.1 = (bf16[2048,1024]{1,0:T(8,128)(2,1)S(1)}, bf16[2048,1024]{1,0:T(8,128)(2,1)}, u32[]{:S(2)}) copy-start(bf16[2048,1024]{1,0:T(8,128)(2,1)} %gather_fusion.1) | copy-start | bytes 12582916
where the time goes:
time: 385 us; the launch traced here: 379 us
  blocking collectives  153 us (40%)
  local copies, waits for them, and re-layouts  108 us (28%)
  waiting for transfers between devices  69.2 us (18%)
  matrix products  23.2 us (6%)
  other arithmetic  16.4 us (4%)
  starting transfers between devices  8.7 us (2%)
    all_to_all x1, blocking collectives, on_device(): lax.all_to_all(outbound_rows, 'blk', split_axis=0, concat_axis=0, tiled=T...  153 us
    all_to_all x1, waiting for transfers between devices, on_device(): lax.all_to_all(lax.all_to_all(outbound_rows, 'blk', split_axis=0, concat_...  69.2 us
    gather x2, local copies, waits for them, and re-layouts, on_device(): normal_rows[source_of]  29.2 us
    dot_general x2, matrix products, masked_tile(): lax.dot_general(left_rows, right_rows, (((1,), (1,)), ((), ())), preferre...  23.2 us
    select_n x1, local copies, waits for them, and re-layouts, on_device(): jnp.where(filled[:, None] == 1, normal_rows[source_of], jnp.zeros((), jnp...  18.8 us
    gather x1, local copies, waits for them, and re-layouts, on_device(): cluster_block = received.reshape(devices * capacity, features)[arrival]  14.6 us
    reshape x1, local copies, waits for them, and re-layouts, on_device(): cluster_block = received.reshape(devices * capacity, features)[arrival]  10.7 us
    all_to_all x1, local copies, waits for them, and re-layouts, on_device(): lax.all_to_all(lax.all_to_all(outbound_rows, 'blk', split_axis=0, concat_...  9.77 us
  transfers between devices with their start and end apart: 2, of which 1 were waited for; matrix products, arithmetic and copies ran while one was open for 3% of the time, Pallas kernels for 0%

commit v1 on v0

v1 whole, which is shorter than its diff:
```python
import math

import jax
import jax.numpy as jnp
import numpy as np
from jax import lax
from jax.experimental import pallas as pl
from jax.experimental.pallas import tpu as pltpu
from jax.sharding import PartitionSpec as P

MESH = pl.DeviceIdType.MESH
ROWS = 2048
FEAT = 1024
CAP = 12
DEV = 256
PLANE = 32
GROUPS = 8
GS = PLANE * CAP
SLOTS = DEV * CAP
WIDE = 256
PARTS = FEAT // WIDE
MR = CAP * PARTS
QUAD = 4 * MR
GR = PLANE * MR
NOBODY = 2.0**23


def swap_matrix():
    r = np.arange(QUAD)
    t, c, w = r // MR, r % MR // CAP, r % CAP
    m = np.zeros((QUAD, QUAD), np.float32)
    m[r, c * MR + t * CAP + w] = 1.0
    return m


def nt(a, b):
    return lax.dot_general(a, b, (((1,), (1,)), ((), ())), preferred_element_type=jnp.float32)


def nn(a, b):
    return jnp.dot(a, b, preferred_element_type=jnp.float32)


def step_dz(i):
    return 4 + (1 - 2 * (i % 2)) * ((i + 1) // 2)


def regroup_kernel(
    emb, ints, swap, out,
    slot_row, sent, got, own, other, hot, rank_col, rank_row, other_rank, best,
    send_sem, recv_sem, pair_send, pair_recv, rank_sem,
):
    blk, x = lax.axis_index("blk"), lax.axis_index("rep")
    z, y, core = blk // 8, (blk // 2) % 4, blk % 2
    me = blk * 4 + x

    def place(z2, d):
        y2 = (y + d // 8) % 4
        c2 = (core + d // 4 % 2) % 2
        x2 = (x + d % 4) % 4
        return z2 * PLANE + y2 * 8 + c2 * 4 + x2, (z2 * 8 + y2 * 2 + c2, x2)

    partner = (z * 8 + y * 2 + (1 - core), x)

    barrier = pltpu.get_barrier_semaphore()

    def greet(k, carry):
        _, device = place((z + k // PLANE) % 8, k % PLANE)
        pl.semaphore_signal(barrier, inc=1, device_id=device, device_id_type=MESH)
        return carry

    lax.fori_loop(1, DEV, greet, 0)

    a = lax.broadcasted_iota(jnp.int32, (256, 512), 0)
    b = lax.broadcasted_iota(jnp.int32, (256, 512), 1)
    prefix = jnp.where((a < b) | (b >= 256), 1.0, 0.0).astype(jnp.bfloat16)
    target_id = lax.broadcasted_iota(jnp.int32, (DEV, 256), 0)
    before = jnp.zeros((DEV, 256), jnp.float32)
    for i in range(ROWS // 256):
        target = ints[0:1, i * 256 : (i + 1) * 256] // ROWS
        one = jnp.where(target_id == target, 1.0, 0.0)
        counts = nn(one.astype(jnp.bfloat16), prefix)
        within = jnp.sum(one * (counts[:, :256] + before), axis=0, keepdims=True)
        before = before + counts[:, 256:]
        slot_row[0:1, i * 256 : (i + 1) * 256] = target * CAP + within.astype(jnp.int32)

    def pack(z2):
        def mark(h, carry):
            ids = lax.broadcasted_iota(jnp.int32, (48, ROWS), 0) + (z2 * GS + h * 48)
            hot[pl.ds(pl.multiple_of(h * 48, 48), 48), :] = jnp.where(
                ids == slot_row[0:1, :], 1.0, 0.0
            ).astype(jnp.bfloat16)
            return carry

        lax.fori_loop(0, GS // 48, mark, 0)
        for c in range(PARTS):
            part = nn(hot[...], emb[:, c * WIDE : (c + 1) * WIDE]).astype(jnp.bfloat16)
            own[0:GS, c * WIDE : (c + 1) * WIDE] = part

        def order(q, carry):
            rows = own[pl.ds(pl.multiple_of(q * 48, 48), 48), :]
            stack = jnp.concatenate([rows[:, c * WIDE : (c + 1) * WIDE] for c in range(PARTS)], axis=0)
            sent[pl.ds(pl.multiple_of(z2 * GR + q * QUAD, QUAD), QUAD), :] = nn(
                swap[...], stack
            ).astype(jnp.bfloat16)
            return carry

        lax.fori_loop(0, GS // 48, order, 0)

    def message(i, z2, d):
        to, device = place(z2, d)
        return pltpu.make_async_remote_copy(
            src_ref=sent.at[pl.ds(pl.multiple_of(to * MR, MR), MR)],
            dst_ref=got.at[pl.ds(pl.multiple_of(me * MR, MR), MR)],
            send_sem=send_sem.at[i],
            recv_sem=recv_sem.at[i],
            device_id=device,
            device_id_type=MESH,
        )

    def send(i, first):
        z2 = (z + step_dz(i)) % 8

        def one(d, carry):
            message(i, z2, d).start()
            return carry

        lax.fori_loop(first, PLANE, one, 0)

    pack((z + step_dz(0)) % 8)
    pl.semaphore_wait(barrier, DEV - 1)
    send(0, 0)

    def pack_and_send(i, carry):
        pack((z + step_dz(i)) % 8)
        send(i, 0)
        return carry

    lax.fori_loop(1, GROUPS - 1, pack_and_send, 0)
    pack(z)
    send(GROUPS - 1, 1)
    mine = pl.ds(pl.multiple_of(me * MR, MR), MR)
    pltpu.make_async_copy(sent.at[mine], got.at[mine], recv_sem.at[GROUPS - 1]).start()

    rank = ints[2:3, :] + 1
    pieces = jnp.concatenate(
        [
            (rank // 65536).astype(jnp.float32),
            (rank // 256 % 256).astype(jnp.float32),
            (rank % 256).astype(jnp.float32),
            jnp.zeros((5, ROWS), jnp.float32),
        ],
        axis=0,
    ).astype(jnp.bfloat16)

    def ranks(i, carry):
        z_src = (z - step_dz(i) + 8) % 8

        def mark(h, carry):
            ids = lax.broadcasted_iota(jnp.int32, (48, ROWS), 0) + (z_src * GS + h * 48)
            hot[pl.ds(pl.multiple_of(h * 48, 48), 48), :] = jnp.where(
                ids == ints[1:2, :], 1.0, 0.0
            ).astype(jnp.bfloat16)
            return carry

        lax.fori_loop(0, GS // 48, mark, 0)
        digits = nt(pieces, hot[...])
        value = digits[0:1] * 65536.0 + digits[1:2] * 256.0 + digits[2:3]
        value = jnp.where(value == 0.0, NOBODY, value)
        rank_row[i] = jnp.broadcast_to(value, (8, GS))
        rank_col[pl.ds(pl.multiple_of(i * GS, GS), GS), :] = jnp.broadcast_to(value, (128, GS)).T
        best[i] = jnp.full((8, GS), -1.0, jnp.float32)
        return carry

    lax.fori_loop(0, GROUPS, ranks, 0)
    rank_copy = pltpu.make_async_remote_copy(
        src_ref=rank_col, dst_ref=other_rank, send_sem=rank_sem.at[0], recv_sem=rank_sem.at[1],
        device_id=partner, device_id_type=MESH,
    )
    rank_copy.start()
    rank_copy.wait_recv()

    def group(i):
        return pl.ds(pl.multiple_of(i * GS, GS), GS)

    def block(rows, row_rank, i, j):
        score = nt(rows[group(i), :], own[group(j), :])
        earlier = row_rank[group(i), :]
        for c in range(GS // 128):
            lanes = slice(c * 128, (c + 1) * 128)
            kept = jnp.where(earlier < rank_row[j, 0:1, lanes], score[:, lanes], -1.0)
            top = jnp.max(kept, axis=0, keepdims=True)
            best[j, :, lanes] = jnp.maximum(best[j, :, lanes], jnp.broadcast_to(top, (8, 128)))

    def pair_copy(i):
        return pltpu.make_async_remote_copy(
            src_ref=own.at[group(i)], dst_ref=other.at[group(i)],
            send_sem=pair_send.at[i], recv_sem=pair_recv.at[i],
            device_id=partner, device_id_type=MESH,
        )

    def step(k, carry):
        z_src = (z - step_dz(k) + 8) % 8
        whole = pl.ds(pl.multiple_of(z_src * GR, GR), GR)
        pltpu.make_async_copy(got.at[whole], got.at[whole], recv_sem.at[k]).wait()

        def take(q, carry):
            rows = nn(swap[...], got[pl.ds(pl.multiple_of(z_src * GR + q * QUAD, QUAD), QUAD), :])
            cols = [rows[c * 48 : (c + 1) * 48, :] for c in range(PARTS)]
            square = cols[0] * cols[0]
            for c in range(1, PARTS):
                square = square + cols[c] * cols[c]
            mean = jnp.sum(square, axis=1, keepdims=True) * (1.0 / FEAT)
            scale = lax.rsqrt(mean + 1e-06) / math.sqrt(FEAT)
            place_rows = pl.ds(pl.multiple_of(k * GS + q * 48, 48), 48)
            for c in range(PARTS):
                own[place_rows, c * WIDE : (c + 1) * WIDE] = (cols[c] * scale).astype(jnp.bfloat16)
            return carry

        lax.fori_loop(0, GS // 48, take, 0)
        pair_copy(k).start()

        def first(j, carry):
            block(own, rank_col, j, k)
            block(other, other_rank, j, k)
            block(own, rank_col, k, j)
            return carry

        lax.fori_loop(0, k, first, 0)
        block(own, rank_col, k, k)
        pair_copy(k).wait_recv()

        def second(j, carry):
            block(other, other_rank, k, j)
            return carry

        lax.fori_loop(0, k + 1, second, 0)
        return carry

    lax.fori_loop(0, GROUPS, step, 0)

    def finish(i, carry):
        z_src = (z - step_dz(i) + 8) % 8
        for c in range(GS // 128):
            out[pl.ds(z_src * 3 + c, 1), :] = best[i, 0:1, c * 128 : (c + 1) * 128]
        pair_copy(i).wait_send()
        return carry

    lax.fori_loop(0, GROUPS, finish, 0)
    rank_copy.wait_send()

    def drain(i, carry):
        part = sent.at[pl.ds(pl.multiple_of(i * GR, GR), GR)]
        pltpu.make_async_copy(part, part, send_sem.at[i]).wait()
        return carry

    lax.fori_loop(0, GROUPS - 1, drain, 0)
    part = sent.at[pl.ds(0, GR - MR)]
    pltpu.make_async_copy(part, part, send_sem.at[GROUPS - 1]).wait()


def regroup(emb, ints, swap):
    vmem = pl.BlockSpec(memory_space=pltpu.VMEM)
    return pl.pallas_call(
        regroup_kernel,
        out_shape=jax.ShapeDtypeStruct((SLOTS // 128, 128), jnp.float32),
        in_specs=[vmem] * 3,
        out_specs=vmem,
        scratch_shapes=[
            pltpu.VMEM((8, ROWS), jnp.int32),
            pltpu.VMEM((DEV * MR, WIDE), jnp.bfloat16),
            pltpu.VMEM((DEV * MR, WIDE), jnp.bfloat16),
            pltpu.VMEM((SLOTS, FEAT), jnp.bfloat16),
            pltpu.VMEM((SLOTS, FEAT), jnp.bfloat16),
            pltpu.VMEM((GS, ROWS), jnp.bfloat16),
            pltpu.VMEM((SLOTS, 128), jnp.float32),
            pltpu.VMEM((GROUPS, 8, GS), jnp.float32),
            pltpu.VMEM((SLOTS, 128), jnp.float32),
            pltpu.VMEM((GROUPS, 8, GS), jnp.float32),
            pltpu.SemaphoreType.DMA((GROUPS,)),
            pltpu.SemaphoreType.DMA((GROUPS,)),
            pltpu.SemaphoreType.DMA((GROUPS,)),
            pltpu.SemaphoreType.DMA((GROUPS,)),
            pltpu.SemaphoreType.DMA((2,)),
        ],
        compiler_params=pltpu.CompilerParams(
            collective_id=0, has_side_effects=True, vmem_limit_bytes=58 * 2**20
        ),
    )(emb, ints, swap)


def pick_kernel(table, arrival, out):
    row, lane = arrival[...] // 128, arrival[...] % 128
    result = jnp.zeros(arrival.shape, jnp.float32)
    for r in range(SLOTS // 128):
        line = jnp.broadcast_to(table[r : r + 1, :], arrival.shape)
        result = jnp.where(row == r, jnp.take_along_axis(line, lane, axis=1), result)
    out[...] = result


def pick(table, arrival):
    return pl.pallas_call(
        pick_kernel, out_shape=jax.ShapeDtypeStruct((ROWS // 128, 128), jnp.float32)
    )(table, arrival.reshape(ROWS // 128, 128)).reshape(ROWS)


def on_device(embeddings, destination, arrival, dataset_index):
    block_id = lax.axis_index("blk") * lax.axis_size("rep") + lax.axis_index("rep")
    rank = lax.dynamic_slice_in_dim(dataset_index, block_id * ROWS, ROWS)
    ints = jnp.stack([destination, arrival, rank])
    table = regroup(embeddings, ints, jnp.asarray(swap_matrix(), jnp.bfloat16))
    return pick(table, arrival)


def solution(mesh):
    placed = (P(("blk", "rep"), None), P(("blk", "rep")), P(("blk", "rep")), P())
    return jax.shard_map(
        on_device, mesh=mesh, in_specs=placed, out_specs=P(("blk", "rep")), check_vma=False
    )
```

time: 385 us -> 219 us (0.57); the launches traced: 379 us -> 219 us
  Pallas kernels: 0 us -> 217 us
  blocking collectives: 153 us -> 0 us
  local copies, waits for them, and re-layouts: 108 us -> 0.7 us
  waiting for transfers between devices: 69.2 us -> 0 us
  matrix products: 23.2 us -> 0 us
  other arithmetic: 16.4 us -> 1.34 us
  starting transfers between devices: 8.7 us -> 0 us
    pallas_call x0 -> x2, Pallas kernels: none -> 217 us  [the longest x1 215 us: regroup(): pl.pallas_call(regroup_kernel, out_shape=jax.ShapeDtypeStruct((SLOTS // 1...]
    all_to_all x1 -> x0, blocking collectives: 153 us -> none  [on_device(): lax.all_to_all(outbound_rows, 'blk', split_axis=0, concat_axis=0, tiled=T...]
    all_to_all x1 -> x0, waiting for transfers between devices: 69.2 us -> none  [on_device(): lax.all_to_all(lax.all_to_all(outbound_rows, 'blk', split_axis=0, concat_...]
    gather x3 -> x0, local copies, waits for them, and re-layouts: 43.8 us -> none  [the longest x2 29.2 us: on_device(): normal_rows[source_of]]
    dot_general x2 -> x0, matrix products: 23.2 us -> none  [masked_tile(): lax.dot_general(left_rows, right_rows, (((1,), (1,)), ((), ())), preferre...]
    select_n x1 -> x0, local copies, waits for them, and re-layouts: 18.8 us -> none  [on_device(): jnp.where(filled[:, None] == 1, normal_rows[source_of], jnp.zeros((), jnp...]
    scatter x2 -> x0, local copies, waits for them, and re-layouts: 16.1 us -> none  [the longest x1 8.06 us: on_device(): source_of = jnp.zeros((devices * capacity,), jnp.int32).at[slot_index].se...]
    all_to_all x2 -> x0, local copies, waits for them, and re-layouts: 16 us -> none  [the longest x1 9.77 us: on_device(): lax.all_to_all(lax.all_to_all(outbound_rows, 'blk', split_axis=0, concat_...]
  transfers between devices with their start and end apart: 2 -> 0, of which waited for: 1 -> 0; matrix products, arithmetic and copies ran while one was open for 3% -> 0% of each run, Pallas kernels for 0% -> 0%
where the time goes in v1:
time: 219 us
  Pallas kernels  217 us (99%)
    pallas_call x1, Pallas kernels, regroup(): pl.pallas_call(regroup_kernel, out_shape=jax.ShapeDtypeStruct((SLOTS // 1...  215 us

profile of v1, /device:TPU:1, one launch (start us, length us, event | category | flops | bytes accessed | tf_op | source)
XLA Modules:
  0.0 218.6 jit_solution(2590361787597951620)
XLA Ops:
  0.0 0.7 dynamic_slice.3
  0.7 1.3 pad_add_fusion.ints
  2.0 215.1 %shard_map.55.table = f32[24,128]{1,0:T(8,128)} custom-call(bf16[2048,1024]{1,0:T(8,128)(2,1)} %emb.1, s32[3,2048]{1,0:T(4,128)} %pad_add_fusion.ints, bf16[192,192]{1,0:T(8,128)(2,1)} %constant.19.clone.swap), custom_call_target="tpu_custom_call" | custom-call | tf_op jit(solution)/shard_map/pallas_call | solution.py:264
  217.2 1.4 shard_map.56

commit v2 on v1

v2 whole, which is shorter than its diff:
```python
import math

import jax
import jax.numpy as jnp
import numpy as np
from jax import lax
from jax.experimental import pallas as pl
from jax.experimental.pallas import tpu as pltpu
from jax.sharding import PartitionSpec as P

MESH = pl.DeviceIdType.MESH
ROWS = 2048
FEAT = 1024
CAP = 12
DEV = 256
PLANE = 32
GROUPS = 8
GS = PLANE * CAP
SLOTS = DEV * CAP
WIDE = 256
PARTS = FEAT // WIDE
MR = CAP * PARTS
QUAD = 4 * MR
GR = PLANE * MR
NOBODY = 2.0**23


def swap_matrix():
    r = np.arange(QUAD)
    t, c, w = r // MR, r % MR // CAP, r % CAP
    m = np.zeros((QUAD, QUAD), np.float32)
    m[r, c * MR + t * CAP + w] = 1.0
    return m


def nt(a, b):
    return lax.dot_general(a, b, (((1,), (1,)), ((), ())), preferred_element_type=jnp.float32)


def nn(a, b):
    return jnp.dot(a, b, preferred_element_type=jnp.float32)


def step_dz(i):
    return 4 + (1 - 2 * (i % 2)) * ((i + 1) // 2)


def regroup_kernel(
    emb, destination, arrival, dataset_index, swap, out,
    rows_in, rank_in, slot_row, sent, got, own, other, hot, rank_col, rank_row, other_rank, best, late,
    in_sem, send_sem, recv_sem, pair_send, pair_recv, rank_sem,
):
    blk, x = lax.axis_index("blk"), lax.axis_index("rep")
    z, y, core = blk // 8, (blk // 2) % 4, blk % 2
    me = blk * 4 + x
    partner = (z * 8 + y * 2 + (1 - core), x)

    def lane_pos(z2, y2, c2, x2):
        return (y2 * 2 + c2) * PLANE + z2 * 4 + x2

    load_rows = pltpu.make_async_copy(emb, rows_in, in_sem.at[0])
    load_rows.start()
    load_rank = pltpu.make_async_copy(
        dataset_index.at[:, pl.ds(pl.multiple_of(me * ROWS, ROWS), ROWS)], rank_in, in_sem.at[1]
    )
    load_rank.start()

    barrier = pltpu.get_barrier_semaphore()

    def greet(k, carry):
        z2, y2 = (z + k // 32) % 8, (y + k // 8) % 4
        c2, x2 = (core + k // 4 % 2) % 2, (x + k % 4) % 4
        pl.semaphore_signal(
            barrier, inc=1, device_id=(z2 * 8 + y2 * 2 + c2, x2), device_id_type=MESH
        )
        return carry

    lax.fori_loop(1, DEV, greet, 0)

    a = lax.broadcasted_iota(jnp.int32, (256, 512), 0)
    b = lax.broadcasted_iota(jnp.int32, (256, 512), 1)
    prefix = jnp.where((a < b) | (b >= 256), 1.0, 0.0).astype(jnp.bfloat16)
    target_id = lax.broadcasted_iota(jnp.int32, (DEV, 256), 0)
    before = jnp.zeros((DEV, 256), jnp.float32)
    for i in range(ROWS // 256):
        target = destination[0:1, i * 256 : (i + 1) * 256] // ROWS
        one = jnp.where(target_id == target, 1.0, 0.0)
        counts = nn(one.astype(jnp.bfloat16), prefix)
        within = jnp.sum(one * (counts[:, :256] + before), axis=0, keepdims=True)
        before = before + counts[:, 256:]
        slot_row[0:1, i * 256 : (i + 1) * 256] = target * CAP + within.astype(jnp.int32)

    def mark(ids_row, y2, c2):
        def one(h, carry):
            ids = lax.broadcasted_iota(jnp.int32, (48, ROWS), 0) + (h * GS + y2 * 96 + c2 * 48)
            hot[pl.ds(pl.multiple_of(h * 48, 48), 48), :] = jnp.where(
                ids == ids_row[0:1, :], 1.0, 0.0
            ).astype(jnp.bfloat16)
            return carry

        lax.fori_loop(0, GS // 48, one, 0)

    def pack(y2, c2):
        mark(slot_row, y2, c2)
        for c in range(PARTS):
            lanes = slice(c * WIDE, (c + 1) * WIDE)
            own[0:GS, lanes] = nn(hot[...], rows_in[:, lanes]).astype(jnp.bfloat16)
        base = (y2 * 2 + c2) * GR
        for q in range(GS // 48):
            stack = jnp.concatenate(
                [own[q * 48 : (q + 1) * 48, c * WIDE : (c + 1) * WIDE] for c in range(PARTS)], axis=0
            )
            sent[pl.ds(pl.multiple_of(base + q * QUAD, QUAD), QUAD), :] = nn(
                swap[...], stack
            ).astype(jnp.bfloat16)

    def message(i, y2, c2, d):
        z2, x2 = (z + step_dz(d % 8)) % 8, (x + 3 - d // 8) % 4
        return pltpu.make_async_remote_copy(
            src_ref=sent.at[pl.ds(pl.multiple_of(lane_pos(z2, y2, c2, x2) * MR, MR), MR)],
            dst_ref=got.at[pl.ds(pl.multiple_of(lane_pos(z, y, core, x) * MR, MR), MR)],
            send_sem=send_sem.at[i],
            recv_sem=recv_sem.at[i],
            device_id=(z2 * 8 + y2 * 2 + c2, x2),
            device_id_type=MESH,
        )

    def send(i, y2, c2, count):
        def one(d, carry):
            message(i, y2, c2, d).start()
            return carry

        lax.fori_loop(0, count, one, 0)

    load_rows.wait()
    pack(y, core)
    pl.semaphore_wait(barrier, DEV - 1)
    send(0, y, core, PLANE - 1)
    mine = pl.ds(pl.multiple_of(lane_pos(z, y, core, x) * MR, MR), MR)
    pltpu.make_async_copy(sent.at[mine], got.at[mine], recv_sem.at[0]).start()

    def pack_and_send(i, carry):
        y2, c2 = (y + i % 4) % 4, (core + i // 4) % 2
        pack(y2, c2)
        send(i, y2, c2, PLANE)
        return carry

    lax.fori_loop(1, GROUPS, pack_and_send, 0)

    load_rank.wait()
    rank = rank_in[...] + 1
    digits = jnp.concatenate(
        [
            jnp.broadcast_to(digit.astype(jnp.float32), (128, ROWS))
            for digit in (rank // 65536, rank // 256 % 256, rank % 256)
        ],
        axis=0,
    ).astype(jnp.bfloat16)

    def source(i):
        return (y + 4 - i % 4) % 4, (core + i // 4) % 2

    def group(i):
        return pl.ds(pl.multiple_of(i * GS, GS), GS)

    def ranks(i, carry):
        mark(arrival, *source(i))
        parts = nt(hot[...], digits)
        value = parts[:, :128] * 65536.0 + parts[:, 128:256] * 256.0 + parts[:, 256:]
        value = jnp.where(value == 0.0, NOBODY, value)
        rank_col[group(i), :] = value
        rank_row[i] = value.T[0:8]
        best[i] = jnp.full((8, GS), -1.0, jnp.float32)
        return carry

    lax.fori_loop(0, GROUPS, ranks, 0)
    rank_copy = pltpu.make_async_remote_copy(
        src_ref=rank_col, dst_ref=other_rank, send_sem=rank_sem.at[0], recv_sem=rank_sem.at[1],
        device_id=partner, device_id_type=MESH,
    )
    rank_copy.start()
    rank_copy.wait_recv()

    def fold(kept):
        return jnp.max(kept.reshape(GS // 8, 8, 128), axis=0)

    def block(rows, row_rank, i, j):
        score = nt(rows[group(i), :], own[group(j), :])
        for c in range(GS // 128):
            lanes = slice(c * 128, (c + 1) * 128)
            earlier = row_rank[group(i), :] < rank_row[j, 0:1, lanes]
            kept = jnp.where(earlier, score[:, lanes], -1.0)
            best[j, :, lanes] = jnp.maximum(best[j, :, lanes], fold(kept))

    def both(i, j):
        score = nt(own[group(i), :], own[group(j), :])
        for c in range(GS // 128):
            lanes = slice(c * 128, (c + 1) * 128)
            earlier = rank_col[group(i), :] < rank_row[j, 0:1, lanes]
            kept = jnp.where(earlier, score[:, lanes], -1.0)
            best[j, :, lanes] = jnp.maximum(best[j, :, lanes], fold(kept))
            late[...] = jnp.maximum(late[...], jnp.where(earlier, -1.0, score[:, lanes]))

    def pair_copy(i):
        return pltpu.make_async_remote_copy(
            src_ref=own.at[group(i)], dst_ref=other.at[group(i)],
            send_sem=pair_send.at[i], recv_sem=pair_recv.at[i],
            device_id=partner, device_id_type=MESH,
        )

    def step(k, carry):
        y2, c2 = source(k)
        base = (y2 * 2 + c2) * GR
        whole = pl.ds(pl.multiple_of(base, GR), GR)
        pltpu.make_async_copy(got.at[whole], got.at[whole], recv_sem.at[k]).wait()
        for q in range(GS // 48):
            rows = nn(swap[...], got[pl.ds(pl.multiple_of(base + q * QUAD, QUAD), QUAD), :])
            cols = [rows[c * 48 : (c + 1) * 48, :] for c in range(PARTS)]
            square = cols[0] * cols[0]
            for c in range(1, PARTS):
                square = square + cols[c] * cols[c]
            mean = jnp.sum(square, axis=1, keepdims=True) * (1.0 / FEAT)
            scale = lax.rsqrt(mean + 1e-06) / math.sqrt(FEAT)
            place_rows = pl.ds(pl.multiple_of(k * GS + q * 48, 48), 48)
            for c in range(PARTS):
                own[place_rows, c * WIDE : (c + 1) * WIDE] = (cols[c] * scale).astype(jnp.bfloat16)
        pair_copy(k).start()
        late[...] = jnp.full((GS, 128), -1.0, jnp.float32)

        def first(j, carry):
            both(k, j)
            block(other, other_rank, j, k)
            return carry

        lax.fori_loop(0, k, first, 0)
        block(own, rank_col, k, k)
        best[k] = jnp.maximum(best[k], jnp.max(late[...].T, axis=0, keepdims=True))
        pair_copy(k).wait_recv()

        def second(j, carry):
            block(other, other_rank, k, j)
            return carry

        lax.fori_loop(0, k + 1, second, 0)
        return carry

    lax.fori_loop(0, GROUPS, step, 0)

    def finish(i, carry):
        y2, c2 = source(i)
        top = jnp.max(best[i], axis=0, keepdims=True)
        for c in range(GS // 128):
            out[pl.ds((y2 * 2 + c2) * 3 + c, 1), :] = top[:, c * 128 : (c + 1) * 128]
        pair_copy(i).wait_send()
        return carry

    lax.fori_loop(0, GROUPS, finish, 0)
    rank_copy.wait_send()

    part = sent.at[pl.ds(0, GR - MR)]
    pltpu.make_async_copy(part, part, send_sem.at[0]).wait()

    def drain(i, carry):
        part = sent.at[pl.ds(pl.multiple_of(i * GR, GR), GR)]
        pltpu.make_async_copy(part, part, send_sem.at[i]).wait()
        return carry

    lax.fori_loop(1, GROUPS, drain, 0)


def regroup(emb, destination, arrival, dataset_index, swap):
    vmem, anywhere = pl.BlockSpec(memory_space=pltpu.VMEM), pl.BlockSpec(memory_space=pl.ANY)
    return pl.pallas_call(
        regroup_kernel,
        out_shape=jax.ShapeDtypeStruct((SLOTS // 128, 128), jnp.float32),
        in_specs=[anywhere, vmem, vmem, anywhere, vmem],
        out_specs=vmem,
        scratch_shapes=[
            pltpu.VMEM((ROWS, FEAT), jnp.bfloat16),
            pltpu.VMEM((1, ROWS), jnp.int32),
            pltpu.VMEM((1, ROWS), jnp.int32),
            pltpu.VMEM((DEV * MR, WIDE), jnp.bfloat16),
            pltpu.VMEM((DEV * MR, WIDE), jnp.bfloat16),
            pltpu.VMEM((SLOTS, FEAT), jnp.bfloat16),
            pltpu.VMEM((SLOTS, FEAT), jnp.bfloat16),
            pltpu.VMEM((GS, ROWS), jnp.bfloat16),
            pltpu.VMEM((SLOTS, 128), jnp.float32),
            pltpu.VMEM((GROUPS, 8, GS), jnp.float32),
            pltpu.VMEM((SLOTS, 128), jnp.float32),
            pltpu.VMEM((GROUPS, 8, GS), jnp.float32),
            pltpu.VMEM((GS, 128), jnp.float32),
            pltpu.SemaphoreType.DMA((2,)),
            pltpu.SemaphoreType.DMA((GROUPS,)),
            pltpu.SemaphoreType.DMA((GROUPS,)),
            pltpu.SemaphoreType.DMA((GROUPS,)),
            pltpu.SemaphoreType.DMA((GROUPS,)),
            pltpu.SemaphoreType.DMA((2,)),
        ],
        compiler_params=pltpu.CompilerParams(
            collective_id=0, has_side_effects=True, vmem_limit_bytes=58 * 2**20
        ),
    )(emb, destination, arrival, dataset_index, swap)


def pick_kernel(table, arrival, out):
    source, rest = arrival[...] // 48, arrival[...] % 48
    column = source // 8 * 48 + rest
    row, lane = source % 8 * 3 + column // 128, column % 128
    result = jnp.zeros(arrival.shape, jnp.float32)
    for r in range(SLOTS // 128):
        line = jnp.broadcast_to(table[r : r + 1, :], arrival.shape)
        result = jnp.where(row == r, jnp.take_along_axis(line, lane, axis=1), result)
    out[...] = result


def pick(table, arrival):
    return pl.pallas_call(
        pick_kernel, out_shape=jax.ShapeDtypeStruct((ROWS // 128, 128), jnp.float32)
    )(table, arrival.reshape(ROWS // 128, 128)).reshape(ROWS)


def on_device(embeddings, destination, arrival, dataset_index):
    table = regroup(
        embeddings,
        destination.reshape(1, ROWS),
        arrival.reshape(1, ROWS),
        dataset_index.reshape(1, -1),
        jnp.asarray(swap_matrix(), jnp.bfloat16),
    )
    return pick(table, arrival)


def solution(mesh):
    placed = (P(("blk", "rep"), None), P(("blk", "rep")), P(("blk", "rep")), P())
    return jax.shard_map(
        on_device, mesh=mesh, in_specs=placed, out_specs=P(("blk", "rep")), check_vma=False
    )
```

time: 219 us -> 174 us (0.79)
  Pallas kernels: 217 us -> 174 us
    pallas_call x1, Pallas kernels: 215 us -> 173 us  [regroup(): pl.pallas_call(regroup_kernel, out_shape=jax.ShapeDtypeStruct((SLOTS // 1...]
where the time goes in v2:
time: 174 us
  Pallas kernels  174 us (100%)
    pallas_call x1, Pallas kernels, regroup(): pl.pallas_call(regroup_kernel, out_shape=jax.ShapeDtypeStruct((SLOTS // 1...  173 us

profile of v2, /device:TPU:1, one launch (start us, length us, event | category | flops | bytes accessed | tf_op | source)
XLA Modules:
  0.0 174.0 jit_solution(6780411869647753952)
XLA Ops:
  0.0 172.5 %shard_map.55.table = f32[24,128]{1,0:T(8,128)} custom-call(bf16[2048,1024]{1,0:T(8,128)(2,1)} %emb.1, s32[1,2048]{1,0:T(1,128)} %bitcast.8, s32[1,2048]{1,0:T(1,128)} %bitcast.6, s32[1,524288]{1,0:T(1,128)} %bitcast.5, bf16[192,192]{1,0:T(8,128)(2,1)} %constant.2.clone.swap), custom_call_target="tpu_custom_call" | custom-call | tf_op jit(solution)/shard_map/pallas_call | solution.py:273
  172.5 1.5 shard_map.56

commit v3 on v2

v3 whole, which is shorter than its diff:
```python
import math

import jax
import jax.numpy as jnp
import numpy as np
from jax import lax
from jax.experimental import pallas as pl
from jax.experimental.pallas import tpu as pltpu
from jax.sharding import PartitionSpec as P

MESH = pl.DeviceIdType.MESH
ROWS = 2048
FEAT = 1024
CAP = 12
DEV = 256
PLANE = 32
GROUPS = 8
GS = PLANE * CAP
SLOTS = DEV * CAP
WIDE = 256
PARTS = FEAT // WIDE
MR = CAP * PARTS
QUAD = 4 * MR
GR = PLANE * MR
LAST = GROUPS - 1
ORDER = (4, 2, 6, 0, 3, 5, 1, 7)
EARLY = 4
PART = (EARLY * 48, (8 - EARLY) * 48)
LANE = (LAST * GS, (LAST + 1) * GS)
LANES = LANE[1] + 256
CHUNK = 512
NOBODY = 2.0**23


def swap_matrix():
    r = np.arange(QUAD)
    t, c, w = r // MR, r % MR // CAP, r % CAP
    m = np.zeros((QUAD, QUAD), np.float32)
    m[r, c * MR + t * CAP + w] = 1.0
    return m


def nt(a, b):
    return lax.dot_general(a, b, (((1,), (1,)), ((), ())), preferred_element_type=jnp.float32)


def nn(a, b):
    return jnp.dot(a, b, preferred_element_type=jnp.float32)


def regroup_kernel(
    emb, destination, arrival, dataset_index, swap, out,
    rows_in, rank_in, slot_row, sent, got, own, other, hot, rank_col, rank_row, other_rank, best, late,
    in_sem, send_sem, recv_sem, pair_send, pair_recv, rank_sem, ready,
):
    blk, x = lax.axis_index("blk"), lax.axis_index("rep")
    z, y, core = blk // 8, (blk // 2) % 4, blk % 2
    me = blk * 4 + x
    partner = (z * 8 + y * 2 + (1 - core), x)

    def lane_pos(z2, y2, c2, x2):
        return (y2 * 2 + c2) * PLANE + z2 * 4 + x2

    load_rows = pltpu.make_async_copy(emb, rows_in, in_sem.at[0])
    load_rows.start()
    load_rank = pltpu.make_async_copy(
        dataset_index.at[:, pl.ds(pl.multiple_of(me * ROWS, ROWS), ROWS)], rank_in, in_sem.at[1]
    )
    load_rank.start()

    barrier = pltpu.get_barrier_semaphore()

    def in_layer(k):
        return lax.rem(z + k // 4, 8) * 8 + y * 2 + core, lax.rem(x + k % 4, 4)

    def in_column(k):
        return z * 8 + lax.rem(y + k // 2, 4) * 2 + lax.rem(core + k % 2, 2), x

    def greet_layer(k, carry):
        pl.semaphore_signal(barrier, inc=1, device_id=in_layer(k), device_id_type=MESH)
        return carry

    def greet_column(k, carry):
        pl.semaphore_signal(barrier, inc=1, device_id=in_column(k), device_id_type=MESH)
        return carry

    lax.fori_loop(1, 32, greet_layer, 0)
    lax.fori_loop(1, 8, greet_column, 0)

    a = lax.broadcasted_iota(jnp.int32, (256, 512), 0)
    b = lax.broadcasted_iota(jnp.int32, (256, 512), 1)
    prefix = jnp.where((a < b) | (b >= 256), 1.0, 0.0).astype(jnp.bfloat16)
    target_id = lax.broadcasted_iota(jnp.int32, (DEV, 256), 0)
    before = jnp.zeros((DEV, 256), jnp.float32)
    for i in range(ROWS // 256):
        target = destination[0:1, i * 256 : (i + 1) * 256] // ROWS
        one = jnp.where(target_id == target, 1.0, 0.0)
        counts = nn(one.astype(jnp.bfloat16), prefix)
        within = jnp.sum(one * (counts[:, :256] + before), axis=0, keepdims=True)
        before = before + counts[:, 256:]
        slot_row[0:1, i * 256 : (i + 1) * 256] = target * CAP + within.astype(jnp.int32)

    def mark_one(ids_row, y2, c2, h, z2):
        ids = lax.broadcasted_iota(jnp.int32, (48, ROWS), 0) + (z2 * GS + y2 * 96 + c2 * 48)
        hot[pl.ds(pl.multiple_of(h * 48, 48), 48), :] = jnp.where(
            ids == ids_row[0:1, :], 1.0, 0.0
        ).astype(jnp.bfloat16)

    def mark(ids_row, y2, c2):
        def one(h, carry):
            mark_one(ids_row, y2, c2, h, h)
            return carry

        lax.fori_loop(0, GS // 48, one, 0)

    def pack(y2, c2):
        mark(slot_row, y2, c2)
        for c in range(PARTS):
            lanes = slice(c * WIDE, (c + 1) * WIDE)
            own[0:GS, lanes] = nn(hot[...], rows_in[:, lanes]).astype(jnp.bfloat16)
        base = (y2 * 2 + c2) * GR
        for q in range(GS // 48):
            stack = jnp.concatenate(
                [own[q * 48 : (q + 1) * 48, c * WIDE : (c + 1) * WIDE] for c in range(PARTS)], axis=0
            )
            sent[pl.ds(pl.multiple_of(base + q * QUAD, QUAD), QUAD), :] = nn(
                swap[...], stack
            ).astype(jnp.bfloat16)

    def message(i, y2, c2, dz, dx):
        z2, x2 = lax.rem(z + dz, 8), lax.rem(x + dx, 4)
        late_part = 1 if dz in ORDER[EARLY:] else 0
        return pltpu.make_async_remote_copy(
            src_ref=sent.at[pl.ds(pl.multiple_of(lane_pos(z2, y2, c2, x2) * MR, MR), MR)],
            dst_ref=got.at[pl.ds(pl.multiple_of(lane_pos(z, y, core, x) * MR, MR), MR)],
            send_sem=send_sem.at[i],
            recv_sem=recv_sem.at[i + i // LAST * late_part],
            device_id=(z2 * 8 + y2 * 2 + c2, x2),
            device_id_type=MESH,
        )

    def send(i, y2, c2, own_layer):
        for dz in ORDER:

            def one(dx, carry, dz=dz):
                message(i, y2, c2, dz, dx).start()
                return carry

            lax.fori_loop(1 if own_layer and dz == 0 else 0, 4, one, 0)

    load_rows.wait()
    pack(y, core)
    pl.semaphore_wait(barrier, 38)
    send(0, y, core, True)

    def tell(k, carry):
        pl.semaphore_signal(ready, inc=1, device_id=in_column(k), device_id_type=MESH)
        return carry

    lax.fori_loop(1, 8, tell, 0)
    mine = pl.ds(pl.multiple_of(lane_pos(z, y, core, x) * MR, MR), MR)
    pltpu.make_async_copy(sent.at[mine], got.at[mine], recv_sem.at[0]).start()
    pl.semaphore_wait(ready, 7)

    def pack_and_send(i, carry):
        y2, c2 = (y + i % 4) % 4, (core + i // 4) % 2
        pack(y2, c2)
        send(i, y2, c2, False)
        return carry

    lax.fori_loop(1, GROUPS, pack_and_send, 0)

    load_rank.wait()
    rank = rank_in[...] + 1
    digits = jnp.concatenate(
        [
            jnp.broadcast_to(digit.astype(jnp.float32), (128, ROWS))
            for digit in (rank // 65536, rank // 256 % 256, rank % 256)
        ],
        axis=0,
    ).astype(jnp.bfloat16)

    def source(i):
        return (y + 4 - i % 4) % 4, (core + i // 4) % 2

    def group(i):
        return pl.ds(pl.multiple_of(i * GS, GS), GS)

    def known(value):
        return jnp.where(value == 0.0, NOBODY, value)

    def columns(rows):
        parts = nt(rows, digits)
        return known(parts[:, :128] * 65536.0 + parts[:, 128:256] * 256.0 + parts[:, 256:])

    def lanes_of(rows):
        parts = [nt(digits[c * 128 : c * 128 + 16], rows) for c in range(3)]
        return known(parts[0] * 65536.0 + parts[1] * 256.0 + parts[2])[0:8]

    def ranks(i, carry):
        mark(arrival, *source(i))
        value = columns(hot[...])
        rank_col[group(i), :] = value
        rank_row[:, group(i)] = value.T[0:8]
        return carry

    lax.fori_loop(0, LAST, ranks, 0)
    for h, dz in enumerate(ORDER):
        mark_one(arrival, *source(LAST), h, lax.rem(z + 8 - dz, 8))
    rank_col[group(LAST), :] = columns(hot[...])
    for s in range(2):
        first_row = s * PART[0]
        rank_row[:, LANE[s] : LANE[s] + PART[s]] = lanes_of(
            hot[first_row : first_row + PART[s], :]
        )
    best[...] = jnp.full((8, LANES), -1.0, jnp.float32)
    rank_copy = pltpu.make_async_remote_copy(
        src_ref=rank_col, dst_ref=other_rank, send_sem=rank_sem.at[0], recv_sem=rank_sem.at[1],
        device_id=partner, device_id_type=MESH,
    )
    rank_copy.start()
    rank_copy.wait_recv()

    def block(rows, row_rank, at, cols, lane, follow=False):
        score = nt(rows[at, :], own[cols, :])
        count, width = score.shape
        for lo in range(0, width, 128):
            w = min(128, width - lo)
            lanes = pl.ds(lane + lo if isinstance(lane, int) else pl.multiple_of(lane + lo, 128), w)
            mine = score[:, lo : lo + w]
            earlier = row_rank[at, :w] < rank_row[0:1, lanes]
            kept = jnp.where(earlier, mine, -1.0)
            top = jnp.max(kept.reshape(count // 8, 8, w), axis=0)
            best[:, lanes] = jnp.maximum(best[:, lanes], top)
            if follow:
                late[:count, :w] = jnp.maximum(late[:count, :w], jnp.where(earlier, -1.0, mine))

    def pair_copy(k, at):
        return pltpu.make_async_remote_copy(
            src_ref=own.at[at], dst_ref=other.at[at],
            send_sem=pair_send.at[k], recv_sem=pair_recv.at[k],
            device_id=partner, device_id_type=MESH,
        )

    def take(row, at):
        rows = nn(swap[...], got[pl.ds(pl.multiple_of(row, QUAD), QUAD), :])
        cols = [rows[c * 48 : (c + 1) * 48, :] for c in range(PARTS)]
        square = cols[0] * cols[0]
        for c in range(1, PARTS):
            square = square + cols[c] * cols[c]
        mean = jnp.sum(square, axis=1, keepdims=True) * (1.0 / FEAT)
        scale = lax.rsqrt(mean + 1e-06) / math.sqrt(FEAT)
        for c in range(PARTS):
            own[pl.ds(pl.multiple_of(at, 48), 48), c * WIDE : (c + 1) * WIDE] = (
                cols[c] * scale
            ).astype(jnp.bfloat16)

    def settle(lane, width):
        lanes = pl.ds(lane, width)
        top = jnp.max(late[...].T, axis=0, keepdims=True)
        best[:, lanes] = jnp.maximum(best[:, lanes], top[:, :width])

    def step(k, carry):
        y2, c2 = source(k)
        base = (y2 * 2 + c2) * GR
        whole = got.at[pl.ds(pl.multiple_of(base, GR), GR)]
        pltpu.make_async_copy(whole, whole, recv_sem.at[k]).wait()
        for q in range(GS // 48):
            take(base + q * QUAD, k * GS + q * 48)
        pair_copy(k, group(k)).start()
        late[...] = jnp.full((GS, 128), -1.0, jnp.float32)

        def first(j, carry):
            block(own, rank_col, group(k), group(j), j * GS, follow=True)
            block(other, other_rank, group(j), group(k), k * GS)
            return carry

        lax.fori_loop(0, k, first, 0)
        block(own, rank_col, group(k), group(k), k * GS)
        settle(pl.multiple_of(k * GS, GS), GS)
        pair_copy(k, group(k)).wait_recv()

        def second(j, carry):
            block(other, other_rank, group(k), group(j), j * GS)
            return carry

        lax.fori_loop(0, k + 1, second, 0)
        return carry

    lax.fori_loop(0, LAST, step, 0)

    parts = [pl.ds(LAST * GS + s * PART[0], PART[s]) for s in range(2)]

    def against_own(rows, row_rank, at, follow):
        def some(j, carry):
            block(rows, row_rank, at, pl.ds(pl.multiple_of(j * CHUNK, CHUNK), CHUNK), j * CHUNK, follow)
            return carry

        whole = LANE[0] // CHUNK
        lax.fori_loop(0, whole, some, 0)
        rest = LANE[0] - whole * CHUNK
        block(rows, row_rank, at, pl.ds(whole * CHUNK, rest), whole * CHUNK, follow)

    y2, c2 = source(LAST)
    base = (y2 * 2 + c2) * GR
    for s in range(2):
        at, k = parts[s], LAST + s
        part = got.at[pl.ds(0, PART[s] * PARTS)]
        pltpu.make_async_copy(part, part, recv_sem.at[k]).wait()
        for q in range(PART[s] // 48):
            z_src = lax.rem(z + 8 - ORDER[s * EARLY + q], 8)
            take(base + z_src * QUAD, LAST * GS + s * PART[0] + q * 48)
        pair_copy(k, at).start()
        late[...] = jnp.full((GS, 128), -1.0, jnp.float32)
        against_own(own, rank_col, at, True)

        def from_other(j, carry):
            block(other, other_rank, group(j), at, LANE[s])
            return carry

        lax.fori_loop(0, LAST, from_other, 0)
        if s == 1:
            block(own, rank_col, at, parts[0], LANE[0], follow=True)
        block(own, rank_col, at, at, LANE[s])
        settle(LANE[s], PART[s])

    for s in range(2):
        pair_copy(LAST + s, parts[s]).wait_recv()
    against_own(other, other_rank, group(LAST), False)
    for s in range(2):
        block(other, other_rank, group(LAST), parts[s], LANE[s])

    top = jnp.max(best[...], axis=0, keepdims=True)
    for r in range(LANES // 128):
        out[r : r + 1, :] = top[:, r * 128 : (r + 1) * 128]

    def close(i, carry):
        pair_copy(i, group(i)).wait_send()
        return carry

    lax.fori_loop(0, LAST, close, 0)
    for s in range(2):
        pair_copy(LAST + s, parts[s]).wait_send()
    rank_copy.wait_send()

    part = sent.at[pl.ds(0, GR - MR)]
    pltpu.make_async_copy(part, part, send_sem.at[0]).wait()

    def drain(i, carry):
        part = sent.at[pl.ds(pl.multiple_of(i * GR, GR), GR)]
        pltpu.make_async_copy(part, part, send_sem.at[i]).wait()
        return carry

    lax.fori_loop(1, GROUPS, drain, 0)


def regroup(emb, destination, arrival, dataset_index, swap):
    vmem, anywhere = pl.BlockSpec(memory_space=pltpu.VMEM), pl.BlockSpec(memory_space=pl.ANY)
    return pl.pallas_call(
        regroup_kernel,
        out_shape=jax.ShapeDtypeStruct((LANES // 128, 128), jnp.float32),
        in_specs=[anywhere, vmem, vmem, anywhere, vmem],
        out_specs=vmem,
        scratch_shapes=[
            pltpu.VMEM((ROWS, FEAT), jnp.bfloat16),
            pltpu.VMEM((1, ROWS), jnp.int32),
            pltpu.VMEM((1, ROWS), jnp.int32),
            pltpu.VMEM((DEV * MR, WIDE), jnp.bfloat16),
            pltpu.VMEM((DEV * MR, WIDE), jnp.bfloat16),
            pltpu.VMEM((SLOTS, FEAT), jnp.bfloat16),
            pltpu.VMEM((SLOTS, FEAT), jnp.bfloat16),
            pltpu.VMEM((GS, ROWS), jnp.bfloat16),
            pltpu.VMEM((SLOTS, 128), jnp.float32),
            pltpu.VMEM((8, LANES), jnp.float32),
            pltpu.VMEM((SLOTS, 128), jnp.float32),
            pltpu.VMEM((8, LANES), jnp.float32),
            pltpu.VMEM((GS, 128), jnp.float32),
            pltpu.SemaphoreType.DMA((2,)),
            pltpu.SemaphoreType.DMA((GROUPS,)),
            pltpu.SemaphoreType.DMA((GROUPS + 1,)),
            pltpu.SemaphoreType.DMA((GROUPS + 1,)),
            pltpu.SemaphoreType.DMA((GROUPS + 1,)),
            pltpu.SemaphoreType.DMA((2,)),
            pltpu.SemaphoreType.REGULAR,
        ],
        compiler_params=pltpu.CompilerParams(
            collective_id=0, has_side_effects=True, vmem_limit_bytes=58 * 2**20
        ),
    )(emb, destination, arrival, dataset_index, swap)


def pick_kernel(table, arrival, out):
    blk = lax.axis_index("blk")
    z, y, core = blk // 8, (blk // 2) % 4, blk % 2
    source, rest = arrival[...] // 48, arrival[...] % 48
    z_src, y_src, c_src = source // 8, source // 2 % 4, source % 2
    step = (y - y_src + 4) % 4 + (c_src - core + 2) % 2 * 4
    lane = step * GS + z_src * 48
    offset = (z - z_src + 8) % 8
    for q, dz in enumerate(ORDER):
        at = LANE[0] + q * 48 if q < EARLY else LANE[1] + (q - EARLY) * 48
        lane = jnp.where((step == LAST) & (offset == dz), at, lane)
    lane = lane + rest
    row, lane = lane // 128, lane % 128
    result = jnp.zeros(arrival.shape, jnp.float32)
    for r in range(LANES // 128):
        line = jnp.broadcast_to(table[r : r + 1, :], arrival.shape)
        result = jnp.where(row == r, jnp.take_along_axis(line, lane, axis=1), result)
    out[...] = result


def pick(table, arrival):
    return pl.pallas_call(
        pick_kernel, out_shape=jax.ShapeDtypeStruct((ROWS // 128, 128), jnp.float32)
    )(table, arrival.reshape(ROWS // 128, 128)).reshape(ROWS)


def on_device(embeddings, destination, arrival, dataset_index):
    table = regroup(
        embeddings,
        destination.reshape(1, ROWS),
        arrival.reshape(1, ROWS),
        dataset_index.reshape(1, -1),
        jnp.asarray(swap_matrix(), jnp.bfloat16),
    )
    return pick(table, arrival)


def solution(mesh):
    placed = (P(("blk", "rep"), None), P(("blk", "rep")), P(("blk", "rep")), P())
    return jax.shard_map(
        on_device, mesh=mesh, in_specs=placed, out_specs=P(("blk", "rep")), check_vma=False
    )
```

time: 174 us -> 167 us (0.960)
  Pallas kernels: 174 us -> 167 us
    pallas_call x1, Pallas kernels: 173 us -> 166 us  [regroup(): pl.pallas_call(regroup_kernel, out_shape=jax.ShapeDtypeStruct((LANES // 1...]
where the time goes in v3:
time: 167 us
  Pallas kernels  167 us (100%)
    pallas_call x1, Pallas kernels, regroup(): pl.pallas_call(regroup_kernel, out_shape=jax.ShapeDtypeStruct((LANES // 1...  166 us

profile of v3, /device:TPU:1, one launch (start us, length us, event | category | flops | bytes accessed | tf_op | source)
XLA Modules:
  0.0 167.2 jit_solution(16667773074765252128)
XLA Ops:
  0.0 165.7 %shard_map.55.table = f32[26,128]{1,0:T(8,128)} custom-call(bf16[2048,1024]{1,0:T(8,128)(2,1)} %emb.1, s32[1,2048]{1,0:T(1,128)} %bitcast.8, s32[1,2048]{1,0:T(1,128)} %bitcast.6, s32[1,524288]{1,0:T(1,128)} %bitcast.5, bf16[192,192]{1,0:T(8,128)(2,1)} %constant.2.clone.swap), custom_call_target="tpu_custom_call" | custom-call | tf_op jit(solution)/shard_map/pallas_call | solution.py:359
  165.7 1.5 shard_map.56
